TPU v7x, 256 devices: a whole 4x4x8 slice. The times are simulated.
256 devices in a mesh: grp: 16 (over x_lo, z), sp: 16 (over y, x_hi, core).
Axes of the slice: x: 4 (x_hi: 2, x_lo: 2; x = x_hi * 2 + x_lo), y: 4, z: 8, core: 2. Of those that a mesh axis runs over, the one named last changes fastest.
Arguments:
- query: bfloat16 [32768, 6144], P(('grp', 'sp')), may hold values from -160 to 160
- key: bfloat16 [32768, 512], P(('grp', 'sp')), may hold values from -160 to 160
- value: bfloat16 [32768, 512], P(('grp', 'sp')), may hold values from -6 to 6
- grad_out: bfloat16 [32768, 6144], P(('grp', 'sp')), may hold values from -64 to 64
- segment_ids: int32 [32768], P(('grp', 'sp')), may hold values from 0 to 63, never falling along the last dimension, each value on 1 to 2048 neighbouring positions
Outputs:
- grad_query: bfloat16 [32768, 6144], P(('grp', 'sp'))
- grad_key: bfloat16 [32768, 512], P(('grp', 'sp'))
- grad_value: bfloat16 [32768, 512], P(('grp', 'sp'))
Inputs may be any that keep to these rules, and one draw needn't show every extreme that they name: `segment_ids`: ids never fall along the tokens; each document (run of one id) has at most 2048 tokens, and one has exactly 2048.
All inputs are finite; a program needn't handle non-finite values.
Results may differ from a plain program's by a relative error of at most 0.012.
Values may be sent and summed in bfloat16 or wider, within the bound.
A program may use at most 128 MiB of HBM per device.

v0:
```python
import jax
import jax.numpy as jnp
from jax import lax
from jax.sharding import PartitionSpec as P

QUERY_HEADS = 48
KEY_VALUE_HEADS = 4
HEAD_SIZE = 128
PACKS = 1
BLOCK_MAX = 512


def block_grads(qb, dob, kw, vw, segq, segk, qpos, kpos, scale):
    f32 = jnp.float32
    score = jnp.einsum("qhd,kd->hqk", qb, kw, preferred_element_type=f32) * scale
    allowed = (segq[:, None] == segk[None, :]) & (kpos[None, :] <= qpos[:, None])
    masked = jnp.where(allowed[None], score, -1e30)
    top = jnp.max(masked, axis=2, keepdims=True)
    expo_total = jnp.sum(jnp.exp(masked - top), axis=2, keepdims=True)
    prob = jnp.exp(masked - top) / expo_total
    prob_low = prob.astype(jnp.bfloat16)
    outs = jnp.einsum("hqk,kd->hqd", prob_low, vw, preferred_element_type=f32)
    delta = jnp.sum(jnp.transpose(dob, (1, 0, 2)).astype(f32) * outs, axis=2)
    value_gradient = jnp.einsum("hqk,qhd->kd", prob_low, dob, preferred_element_type=f32)
    dprob = jnp.einsum("qhd,kd->hqk", dob, vw, preferred_element_type=f32)
    dscore = (jnp.exp(masked - top) / expo_total * (dprob - delta[:, :, None])).astype(jnp.bfloat16)
    grad_q = jnp.einsum("hqk,kd->qhd", dscore, kw, preferred_element_type=f32) * scale
    key_gradient = jnp.einsum("hqk,qhd->kd", dscore, qb, preferred_element_type=f32) * scale
    return (grad_q, key_gradient, value_gradient)


def window_pass(q_seq, d_seq, k_seq, v_seq, seg_seq, pack_len, block):
    sequence_input = q_seq.shape[0]
    scale = HEAD_SIZE ** (-0.5)
    key_gradient = jnp.zeros((sequence_input, HEAD_SIZE), jnp.float32)
    value_gradient = jnp.zeros((sequence_input, HEAD_SIZE), jnp.float32)
    pieces = []
    for index in range(pack_len // block):
        start = index * block
        finish = start + block
        qpos = start + jnp.arange(block, dtype=jnp.int32)
        kpos = 0 + jnp.arange(finish, dtype=jnp.int32)
        piece_q, piece_k, piece_v = block_grads(
            q_seq[start:finish],
            d_seq[start:finish],
            k_seq[0:finish],
            v_seq[0:finish],
            seg_seq[start:finish],
            seg_seq[0:finish],
            qpos,
            kpos,
            scale,
        )
        pieces.append(piece_q)
        key_gradient = key_gradient.at[0:finish].add(piece_k)
        value_gradient = value_gradient.at[0:finish].add(piece_v)
    grad_q = jnp.concatenate(pieces, axis=0)
    return (grad_q, key_gradient, value_gradient)


def on_device(query, key, value, grad_out, segment_ids):
    model_width = lax.axis_size("sp")
    heads_here = QUERY_HEADS // model_width
    repeat_factor = model_width // KEY_VALUE_HEADS
    row_count = query.shape[0]
    sequence_input = row_count * model_width
    pack_len = sequence_input // PACKS
    block = min(BLOCK_MAX, pack_len)
    q_split = query.reshape(row_count, model_width, heads_here, HEAD_SIZE)
    d_split = grad_out.reshape(row_count, model_width, heads_here, HEAD_SIZE)
    q_seq, d_seq = (
        lax.all_to_all(q_split, "sp", split_axis=1, concat_axis=0, tiled=True),
        lax.all_to_all(d_split, "sp", split_axis=1, concat_axis=0, tiled=True),
    )
    k_whole, v_whole = (
        lax.all_gather(key, "sp", axis=0, tiled=True),
        lax.all_gather(value, "sp", axis=0, tiled=True),
    )
    offset = lax.axis_index("sp") // repeat_factor * HEAD_SIZE
    k_seq = lax.dynamic_slice_in_dim(k_whole, offset, HEAD_SIZE, 1)
    v_seq = lax.dynamic_slice_in_dim(v_whole, offset, HEAD_SIZE, 1)
    q_seq = q_seq.reshape(sequence_input, heads_here, HEAD_SIZE)
    d_seq = d_seq.reshape(sequence_input, heads_here, HEAD_SIZE)
    seg_seq = lax.all_gather(segment_ids, "sp", axis=0, tiled=True)
    grad_q, key_gradient, value_gradient = window_pass(
        q_seq, d_seq, k_seq, v_seq, seg_seq, pack_len, block
    )
    q_low = grad_q.astype(jnp.bfloat16).reshape(sequence_input, 1, heads_here, HEAD_SIZE)
    k_low = key_gradient.astype(jnp.bfloat16).reshape(sequence_input, 1, 1, HEAD_SIZE)
    v_low = value_gradient.astype(jnp.bfloat16).reshape(sequence_input, 1, 1, HEAD_SIZE)
    q_back, k_back, v_back = (
        lax.all_to_all(q_low, "sp", split_axis=0, concat_axis=1, tiled=True),
        lax.all_to_all(k_low, "sp", split_axis=0, concat_axis=1, tiled=True),
        lax.all_to_all(v_low, "sp", split_axis=0, concat_axis=1, tiled=True),
    )
    q_final = q_back.reshape(row_count, QUERY_HEADS * HEAD_SIZE).astype(jnp.float32)
    k_final = (
        k_back.astype(jnp.float32)
        .reshape(row_count, KEY_VALUE_HEADS, repeat_factor, HEAD_SIZE)
        .sum(axis=2)
        .reshape(row_count, KEY_VALUE_HEADS * HEAD_SIZE)
    )
    v_final = (
        v_back.astype(jnp.float32)
        .reshape(row_count, KEY_VALUE_HEADS, repeat_factor, HEAD_SIZE)
        .sum(axis=2)
        .reshape(row_count, KEY_VALUE_HEADS * HEAD_SIZE)
    )
    local = jnp.sum(q_final * q_final) + jnp.sum(k_final * k_final) + jnp.sum(v_final * v_final)
    total = lax.psum(local, ("grp", "sp"))
    item_count = float(
        row_count
        * model_width
        * lax.axis_size("grp")
        * (QUERY_HEADS + 2 * KEY_VALUE_HEADS)
        * HEAD_SIZE
    )
    rms = jnp.sqrt(total / item_count + 1e-06)
    return (
        (q_final / rms).astype(jnp.bfloat16),
        (k_final / rms).astype(jnp.bfloat16),
        (v_final / rms).astype(jnp.bfloat16),
    )


def solution(mesh):
    return jax.shard_map(
        on_device,
        mesh=mesh,
        in_specs=(
            P(("grp", "sp"), None),
            P(("grp", "sp"), None),
            P(("grp", "sp"), None),
            P(("grp", "sp"), None),
            P(("grp", "sp")),
        ),
        out_specs=(P(("grp", "sp"), None), P(("grp", "sp"), None), P(("grp", "sp"), None)),
        check_vma=False,
    )
```

profile of v0, /device:TPU:1, one launch (start us, length us, event | category | flops | bytes accessed | tf_op | source)
XLA Modules:
  0.0 388.1 jit_solution(16270957007236123803)
XLA Ops:
  7.9 2.7 copy.97
  10.6 8.6 %all-to-all-start = ((bf16[128,16,3,128]{0,3,2,1:T(8,128)(2,1)}), bf16[128,16,3,128]{0,3,2,1:T(8,128)(2,1)S(1)}, u32[]{:S(2)}, u32[]{:S(2)}) async-start(bf16[128,16,3,128]{0,3,2,1:T(8,128)(2,1)} %bitcast.4), calls=%async_computation | async-start | bytes 3145728 | tf_op jit(solution)/shard_map/all_to_all | solution.py:72
  19.9 1.6 copy.99
  21.5 35.2 %all-gather = s32[16,1,128]{2,1,0:T(1,128)S(1)} all-gather(s32[1,1,128]{2,1,0:T(1,128)S(1)} %bitcast.332), channel_id=1, replica_groups=mesh['grp'=16,'sp'=16] {'sp'}, dimensions={0}, use_global_device_ids=true | all-gather | bytes 8704 | tf_op jit(solution)/shard_map/all_gather | solution.py:84
  57.6 3.7 all-to-all-start.1
  64.2 2.0 fusion.20
  67.3 1.9 copy.98
  71.4 2.0 copy.106
  73.4 10.9 %all-to-all-done.1 = bf16[128,16,3,128]{0,3,2,1:T(8,128)(2,1)S(1)} async-done(((bf16[128,16,3,128]{0,3,2,1:T(8,128)(2,1)}), bf16[128,16,3,128]{0,3,2,1:T(8,128)(2,1)S(1)}, u32[]{:S(2)}, u32[]{:S(2)}) %all-to-all-start.1) | async-done | bytes 1572896 | tf_op jit(solution)/shard_map/all_to_all | solution.py:73
  86.9 3.8 fusion.137
  90.7 2.3 fusion.50
  93.5 43.6 %all-gather.6.cloned.1.call-done = bf16[2048,512]{1,0:T(8,128)(2,1)} async-done(((bf16[128,512]{1,0:T(8,128)(2,1)}), bf16[2048,512]{1,0:T(8,128)(2,1)}) %all-gather.6.cloned.1.call-update) | async-done | bytes 2097168 | tf_op jit(solution)/shard_map/all_gather | solution.py:77
  137.2 1.7 fusion.60
  138.8 2.5 fusion.25
  143.7 6.1 %fusion.136 = (f32[3,512]{1,0:T(4,128)S(1)}, f32[3,512,1024]{1,2,0:T(8,128)}) fusion(pred[512,1024]{0,1:T(8,128)(4,1)} %fusion.44, bf16[512,3,128]{2,0,1:T(8,128)(2,1)S(1)} %bitcast.310, bf16[2048,512]{1,0:T(8,128)(2,1)} %all-gather.4.cloned.1.call-done, s32[]{:T(128)S(6)} %select_n.26), kind=kOutput, calls=%fused_computation.170 | convolution fusion | flops 408945664 | bytes 7477252 | tf_op jit(solution)/shard_map/sub | solution.py:26
  149.8 3.8 fusion.30
  154.7 2.3 fusion.61
  157.1 2.0 fusion.11
  159.1 3.8 fusion.57
  162.9 2.4 fusion.91
  165.3 8.3 %fusion.135 = (f32[3,512]{1,0:T(4,128)S(1)}, f32[3,512,1536]{1,2,0:T(8,128)}) fusion(f32[1536,512,3]{1,0,2:T(8,128)S(1)} %fusion.91, pred[512,1536]{0,1:T(8,128)(4,1)} %fusion.28), kind=kOutput, calls=%fused_computation.169 | output fusion | flops 14157311 | bytes 19666944 | tf_op jit(solution)/shard_map/sub | solution.py:26
  173.5 5.2 %fusion.21 = bf16[3,512,1536]{1,2,0:T(8,128)(2,1)S(1)} fusion(f32[3,512,1536]{1,2,0:T(8,128)} %get-tuple-element.139, f32[3,512]{1,0:T(4,128)S(1)} %get-tuple-element.138), kind=kLoop, calls=%fused_computation.35 | loop fusion | flops 4718592 | bytes 14161920 | tf_op jit(solution)/shard_map/convert_element_type | solution.py:21
  180.3 2.9 fusion.62
  183.2 3.0 fusion.8
  186.2 4.2 %fusion.34 = f32[2048,128]{1,0:T(8,128)} fusion(f32[2048,128]{1,0:T(8,128)} %fusion.57, bf16[3,512,1536]{1,2,0:T(8,128)(2,1)S(1)} %fusion.8, bf16[512,3,128]{2,0,1:T(8,128)(2,1)S(1)} %bitcast.302), kind=kOutput, calls=%fused_computation.57 | convolution fusion | flops 604372992 | bytes 6684672 | tf_op jit(solution)/shard_map/hqk,qhd->kd/dot_general | solution.py:28
  190.5 10.4 %fusion.130 = (f32[3,512]{1,0:T(4,128)S(1)}, f32[3,512,2048]{1,2,0:T(8,128)}) fusion(pred[512,2048]{0,1:T(8,128)(4,1)S(1)} %copy-done.18, bf16[512,3,128]{2,0,1:T(8,128)(2,1)S(1)} %bitcast.305, bf16[2048,512]{1,0:T(8,128)(2,1)} %all-gather.4.cloned.1.call-done, s32[]{:T(128)S(6)} %select_n.26), kind=kOutput, calls=%fused_computation.168 | convolution fusion | flops 817891328 | bytes 14555140 | tf_op jit(solution)/shard_map/sub | solution.py:26
  200.8 6.4 %fusion.15 = bf16[3,512,2048]{1,2,0:T(8,128)(2,1)S(1)} fusion(f32[3,512,2048]{1,2,0:T(8,128)} %get-tuple-element.137, f32[3,512]{1,0:T(4,128)S(1)} %get-tuple-element.136), kind=kLoop, calls=%fused_computation.25 | loop fusion | flops 6291456 | bytes 18880512 | tf_op jit(solution)/shard_map/convert_element_type | solution.py:21
  207.3 4.0 %fusion.43 = bf16[2048,1,1,128]{3,0,2,1:T(8,128)(2,1)} fusion(f32[2048,128]{1,0:T(8,128)} %copy-done.6, bf16[3,512,2048]{1,2,0:T(8,128)(2,1)S(1)} %fusion.15, bf16[512,3,128]{2,0,1:T(8,128)(2,1)S(1)} %bitcast.307), kind=kOutput, calls=%fused_computation.66 | convolution fusion | flops 805830656 | bytes 8257536 | tf_op jit(solution)/shard_map/hqk,qhd->kd/dot_general | solution.py:24
  211.2 2.0 fusion.63
  213.2 5.9 %fusion.5 = bf16[3,512,2048]{1,2,0:T(8,128)(2,1)S(1)} fusion(f32[3,512]{1,0:T(4,128)S(1)} %fusion.63, bf16[512,3,128]{2,0,1:T(8,128)(2,1)S(1)} %bitcast.309, f32[3,512,2048]{1,2,0:T(8,128)} %get-tuple-element.137, f32[3,512]{1,0:T(4,128)S(1)} %get-tuple-element.136, bf16[2048,512]{1,0:T(8,128)(2,1)S(1)} %copy-done.21, s32[]{:T(128)S(6)} %select_n.26), kind=kOutput, calls=%fused_computation.6 | convolution fusion | flops 817889280 | bytes 19808260 | tf_op jit(solution)/shard_map/qhd,kd->hqk/dot_general | solution.py:25
  219.2 2.7 copy-done.1
  221.8 3.1 fusion.42
  227.4 4.2 %all-to-all-start.3 = ((bf16[16,2,8192]{2,1,0:T(2,128)(2,1)}), bf16[16,2,8192]{2,1,0:T(2,128)(2,1)}, u32[]{:S(2)}, u32[]{:S(2)}) async-start(bf16[16,2,8192]{2,1,0:T(2,128)(2,1)} %reshape.565), calls=%async_computation.3 | async-start | bytes 1048576 | tf_op jit(solution)/shard_map/all_to_all | solution.py:93
  231.6 3.3 fusion.64
  236.9 4.9 %fusion.66 = bf16[512,1,3,128]{0,3,2,1:T(8,128)(2,1)} fusion(bf16[3,512,2048]{1,2,0:T(8,128)(2,1)} %copy-done.1, bf16[2048,512]{1,0:T(8,128)(2,1)} %all-gather.4.cloned.1.call-done, s32[]{:T(128)S(6)} %select_n.26), kind=kOutput, calls=%fused_computation.101 | convolution fusion | flops 805699584 | bytes 7208964 | tf_op jit(solution)/shard_map/hqk,kd->qhd/dot_general | solution.py:27
  243.1 6.0 %all-to-all-start.4 = ((bf16[16,2,8192]{2,1,0:T(2,128)(2,1)}), bf16[16,2,8192]{2,1,0:T(2,128)(2,1)}, u32[]{:S(2)}, u32[]{:S(2)}) async-start(bf16[16,2,8192]{2,1,0:T(2,128)(2,1)} %reshape.567), calls=%async_computation.4 | async-start | bytes 1048576 | tf_op jit(solution)/shard_map/all_to_all | solution.py:94
  249.1 1.7 fusion.65
  252.3 2.5 copy.127
  254.9 5.6 %all-to-all-done.4 = bf16[16,2,8192]{2,1,0:T(2,128)(2,1)} async-done(((bf16[16,2,8192]{2,1,0:T(2,128)(2,1)}), bf16[16,2,8192]{2,1,0:T(2,128)(2,1)}, u32[]{:S(2)}, u32[]{:S(2)}) %all-to-all-start.4) | async-done | bytes 524320 | tf_op jit(solution)/shard_map/all_to_all | solution.py:94
  260.5 4.7 %all-to-all-start.2 = ((bf16[2048,1,3,128]{3,2,1,0:T(4,128)(2,1)}), bf16[2048,1,3,128]{3,2,1,0:T(4,128)(2,1)S(1)}, u32[]{:S(2)}, u32[]{:S(2)}) async-start(bf16[2048,1,3,128]{3,2,1,0:T(4,128)(2,1)} %copy.127), calls=%async_computation.2 | async-start | bytes 4194304 | tf_op jit(solution)/shard_map/all_to_all | solution.py:92
  265.1 2.2 reshape.568
  267.4 1.9 convert_element_type.170
  270.6 3.5 reshape.566
  274.0 2.2 convert_element_type.169
  277.7 1.6 multiply_reduce_fusion.1
  279.3 14.4 %all-to-all-done.2 = bf16[2048,1,3,128]{3,2,1,0:T(4,128)(2,1)S(1)} async-done(((bf16[2048,1,3,128]{3,2,1,0:T(4,128)(2,1)}), bf16[2048,1,3,128]{3,2,1,0:T(4,128)(2,1)S(1)}, u32[]{:S(2)}, u32[]{:S(2)}) %all-to-all-start.2) | async-done | bytes 1572896 | tf_op jit(solution)/shard_map/all_to_all | solution.py:92
  297.0 75.6 %psum.7 = f32[]{:T(128)} all-reduce(f32[]{:T(128)S(6)} %add.120), channel_id=1, replica_groups=mesh['grp'=16,'sp'=16] {'grp','sp'}, use_global_device_ids=true, to_apply=%region_17.18 | all-reduce | flops 1 | bytes 8 | tf_op jit(solution)/shard_map/psum | solution.py:110
  376.6 1.9 copy.131
  (103 shorter events, 33.6 us)
Async XLA Ops:
  7.2 79.7 %all-gather.4.cloned.1.call-start = ((), (), s32[]{:S(2)}) async-start(), calls=%async_computation.5 | async-start | bytes 2228224 | tf_op jit(solution)/shard_map/all_gather | solution.py:76
  7.9 12.0 %copy-start.14 = (bf16[128,6144]{1,0:T(8,128)(2,1)S(1)}, bf16[128,6144]{1,0:T(8,128)(2,1)}, u32[]{:S(2)}) copy-start(bf16[128,6144]{1,0:T(8,128)(2,1)} %param.28) | copy-start | bytes 4718596
  10.6 10.9 %copy-start.20 = (s32[128]{0:T(128)S(1)}, s32[128]{0:T(128)}, u32[]{:S(2)}) copy-start(s32[128]{0:T(128)} %param.29) | copy-start | bytes 1540
  10.6 47.0 %all-to-all-start = ((bf16[128,16,3,128]{0,3,2,1:T(8,128)(2,1)}), bf16[128,16,3,128]{0,3,2,1:T(8,128)(2,1)S(1)}, u32[]{:S(2)}, u32[]{:S(2)}) async-start(bf16[128,16,3,128]{0,3,2,1:T(8,128)(2,1)} %bitcast.4), calls=%async_computation | async-start | bytes 3145728 | tf_op jit(solution)/shard_map/all_to_all | solution.py:72
  19.2 118.0 %all-gather.6.cloned.1.call-start = ((), (), s32[]{:S(2)}) async-start(), calls=%async_computation.6 | async-start | bytes 2228224 | tf_op jit(solution)/shard_map/all_gather | solution.py:77
  57.6 26.6 %all-to-all-start.1 = ((bf16[128,16,3,128]{0,3,2,1:T(8,128)(2,1)}), bf16[128,16,3,128]{0,3,2,1:T(8,128)(2,1)S(1)}, u32[]{:S(2)}, u32[]{:S(2)}) async-start(bf16[128,16,3,128]{0,3,2,1:T(8,128)(2,1)} %bitcast.10), calls=%async_computation.1 | async-start | bytes 3145728 | tf_op jit(solution)/shard_map/all_to_all | solution.py:73
  84.5 2.4 copy-start.16
  84.5 2.4 copy-start.19
  141.4 1.1 copy-start.7
  141.4 2.3 copy-start.15
  149.8 7.2 %slice-start.3 = ((s8[6291456]{0:T(1024)(128)(4,1)}), s8[4194304]{0:T(1024)(128)(4,1)S(1)}, s32[]{:S(2)}) async-start(s8[6291456]{0:T(1024)(128)(4,1)} %bitcast.299), calls=%async_computation.10 | async-start | bytes 8388608
  153.7 3.4 slice-start.4
  154.7 4.4 %copy-start.4 = (f32[2048,128]{1,0:T(8,128)}, f32[2048,128]{1,0:T(8,128)S(1)}, u32[]{:S(2)}) copy-start(f32[2048,128]{1,0:T(8,128)S(1)} %fusion.59) | copy-start | bytes 3145732
  159.0 3.8 copy-start.2
  173.5 5.3 %copy-start.5 = (f32[2048,128]{1,0:T(8,128)S(1)}, f32[2048,128]{1,0:T(8,128)}, u32[]{:S(2)}) copy-start(f32[2048,128]{1,0:T(8,128)} %copy-done.4) | copy-start | bytes 3145732
  173.5 5.3 %copy-start.17 = (bf16[4,128,1,3,128]{4,1,0,3,2:T(8,128)(2,1)S(1)}, bf16[4,128,1,3,128]{4,1,0,3,2:T(8,128)(2,1)}, u32[]{:S(2)}) copy-start(bf16[4,128,1,3,128]{4,1,0,3,2:T(8,128)(2,1)} %copy.114) | copy-start | bytes 1179652
  173.5 9.7 %slice-start = ((s8[9437184]{0:T(1024)(128)(4,1)}), s8[4194304]{0:T(1024)(128)(4,1)S(1)}, s32[]{:S(2)}) async-start(s8[9437184]{0:T(1024)(128)(4,1)} %bitcast.293), calls=%async_computation.7 | async-start | bytes 8388608
  173.5 9.7 %slice-start.1 = ((s8[9437184]{0:T(1024)(128)(4,1)}), s8[4194304]{0:T(1024)(128)(4,1)S(1)}, s32[]{:S(2)}) async-start(s8[9437184]{0:T(1024)(128)(4,1)} %bitcast.293), calls=%async_computation.8 | async-start | bytes 8388608
  178.8 4.4 %slice-start.2 = ((s8[9437184]{0:T(1024)(128)(4,1)}), s8[1048576]{0:T(1024)(128)(4,1)S(1)}, s32[]{:S(2)}) async-start(s8[9437184]{0:T(1024)(128)(4,1)} %bitcast.293), calls=%async_computation.9 | async-start | bytes 2097152
  180.3 6.0 %copy-start.6 = (f32[2048,128]{1,0:T(8,128)}, f32[2048,128]{1,0:T(8,128)S(1)}, u32[]{:S(2)}) copy-start(f32[2048,128]{1,0:T(8,128)S(1)} %fusion.36) | copy-start | bytes 3145732
  186.2 4.2 %copy-start = (bf16[3,512,1536]{1,2,0:T(8,128)(2,1)}, bf16[3,512,1536]{1,2,0:T(8,128)(2,1)S(1)}, u32[]{:S(2)}) copy-start(bf16[3,512,1536]{1,2,0:T(8,128)(2,1)S(1)} %fusion.8) | copy-start | bytes 14155780
  186.2 4.2 %copy-start.11 = (bf16[4,128,1,3,128]{4,1,0,3,2:T(8,128)(2,1)S(1)}, bf16[4,128,1,3,128]{4,1,0,3,2:T(8,128)(2,1)}, u32[]{:S(2)}) copy-start(bf16[4,128,1,3,128]{4,1,0,3,2:T(8,128)(2,1)} %copy.120) | copy-start | bytes 1179652
  186.2 4.2 %copy-start.18 = (pred[512,2048]{0,1:T(8,128)(4,1)S(1)}, pred[512,2048]{0,1:T(8,128)(4,1)}, u32[]{:S(2)}) copy-start(pred[512,2048]{0,1:T(8,128)(4,1)} %fusion.20) | copy-start | bytes 3145732
  200.8 6.4 %copy-start.13 = (bf16[4,128,1,3,128]{4,1,0,3,2:T(8,128)(2,1)S(1)}, bf16[4,128,1,3,128]{4,1,0,3,2:T(8,128)(2,1)}, u32[]{:S(2)}) copy-start(bf16[4,128,1,3,128]{4,1,0,3,2:T(8,128)(2,1)} %copy.121) | copy-start | bytes 1179652
  207.3 4.0 %copy-start.21 = (bf16[2048,512]{1,0:T(8,128)(2,1)S(1)}, bf16[2048,512]{1,0:T(8,128)(2,1)}, u32[]{:S(2)}) copy-start(bf16[2048,512]{1,0:T(8,128)(2,1)} %all-gather.6.cloned.1.call-done) | copy-start | bytes 6291460
  213.2 8.6 %copy-start.12 = (bf16[4,128,1,3,128]{4,1,0,3,2:T(8,128)(2,1)S(1)}, bf16[4,128,1,3,128]{4,1,0,3,2:T(8,128)(2,1)}, u32[]{:S(2)}) copy-start(bf16[4,128,1,3,128]{4,1,0,3,2:T(8,128)(2,1)} %copy.120) | copy-start | bytes 1179652
  219.1 2.7 copy-start.1
  227.4 15.7 %all-to-all-start.3 = ((bf16[16,2,8192]{2,1,0:T(2,128)(2,1)}), bf16[16,2,8192]{2,1,0:T(2,128)(2,1)}, u32[]{:S(2)}, u32[]{:S(2)}) async-start(bf16[16,2,8192]{2,1,0:T(2,128)(2,1)} %reshape.565), calls=%async_computation.3 | async-start | bytes 1048576 | tf_op jit(solution)/shard_map/all_to_all | solution.py:93
  231.6 3.4 copy-start.9
  236.9 12.2 %copy-start.3 = (bf16[3,512,1024]{1,2,0:T(8,128)(2,1)S(1)}, bf16[3,512,1024]{1,2,0:T(8,128)(2,1)}, u32[]{:S(2)}) copy-start(bf16[3,512,1024]{1,2,0:T(8,128)(2,1)} %copy-done.2) | copy-start | bytes 9437188
  243.1 17.4 %all-to-all-start.4 = ((bf16[16,2,8192]{2,1,0:T(2,128)(2,1)}), bf16[16,2,8192]{2,1,0:T(2,128)(2,1)}, u32[]{:S(2)}, u32[]{:S(2)}) async-start(bf16[16,2,8192]{2,1,0:T(2,128)(2,1)} %reshape.567), calls=%async_computation.4 | async-start | bytes 1048576 | tf_op jit(solution)/shard_map/all_to_all | solution.py:94
  249.1 1.7 copy-start.8
  249.1 3.0 copy-start.10
  260.5 33.2 %all-to-all-start.2 = ((bf16[2048,1,3,128]{3,2,1,0:T(4,128)(2,1)}), bf16[2048,1,3,128]{3,2,1,0:T(4,128)(2,1)S(1)}, u32[]{:S(2)}, u32[]{:S(2)}) async-start(bf16[2048,1,3,128]{3,2,1,0:T(4,128)(2,1)} %copy.127), calls=%async_computation.2 | async-start | bytes 4194304 | tf_op jit(solution)/shard_map/all_to_all | solution.py:92
Sparse Core Ops, SparseCore 0:
  10.8 71.3 all-gather.3
  84.9 52.2 all-gather.5
where the time goes:
time: 393 us; the launch traced here: 388 us
  blocking collectives  111 us (28%)
  waiting for transfers between devices  77.2 us (20%)
  matrix products  74.8 us (19%)
  other arithmetic  46.3 us (12%)
  local copies, waits for them, and re-layouts  34.3 us (9%)
  starting transfers between devices  27.2 us (7%)
  between operations  17.5 us (4%)
    psum x1, blocking collectives, on_device(): total = lax.psum(local, ('grp', 'sp'))  75.6 us
    all_gather x1, waiting for transfers between devices, on_device(): lax.all_gather(value, 'sp', axis=0, tiled=True)  43.6 us
    all_gather x1, blocking collectives, on_device(): seg_seq = lax.all_gather(segment_ids, 'sp', axis=0, tiled=True)  35.2 us
    sub x3, matrix products, block_grads(): masked - top  20.3 us
    unnamed x63, local copies, waits for them, and re-layouts  18.3 us
    convert_element_type x4, other arithmetic, block_grads(): prob_low = prob.astype(jnp.bfloat16)  17.8 us
    all_to_all x1, waiting for transfers between devices, on_device(): lax.all_to_all(q_low, 'sp', split_axis=0, concat_axis=1, tiled=True)  14.4 us
    dot_general x4, matrix products, block_grads(): dprob = jnp.einsum('qhd,kd->hqk', dob, vw, preferred_element_type=f32)  13.4 us
  transfers between devices with their start and end apart: 7, of which 5 were waited for; matrix products, arithmetic and copies ran while one was open for 15% of the time, Pallas kernels for 0%

commit v1 on v0

v1 whole, which is shorter than its diff:
```python
import functools

import jax
import jax.numpy as jnp
from jax import lax
from jax.experimental import pallas as pl
from jax.experimental.pallas import tpu as pltpu
from jax.sharding import PartitionSpec as P

QUERY_HEADS = 48
KEY_VALUE_HEADS = 4
HEAD_SIZE = 128
TOK = 128
N_SP = 16
N_GRP = 16
ROWS = 2 * TOK
SEQ = TOK * N_SP
HALF_Q = QUERY_HEADS * HEAD_SIZE // 2
HALF_KV = KEY_VALUE_HEADS * HEAD_SIZE // 2
CORE_HEADS = QUERY_HEADS // 2
GROUP_HEADS = QUERY_HEADS // KEY_VALUE_HEADS
SCALE = HEAD_SIZE**-0.5
EXP2_SCALE = SCALE * 1.4426950408889634
NEG = -1e30
HB = 4
KB = 256
WIDE = HB * ROWS
ITEMS = float(TOK * N_SP * N_GRP * (QUERY_HEADS + 2 * KEY_VALUE_HEADS) * HEAD_SIZE)

f32 = jnp.float32
bf16 = jnp.bfloat16
MESH = pl.DeviceIdType.MESH


def greet(axis, me, count):
    barrier = pltpu.get_barrier_semaphore()

    def one(d, z):
        other = lax.rem(me + d, count)
        pl.semaphore_signal(barrier, inc=1, device_id={axis: other}, device_id_type=MESH)
        return z

    lax.fori_loop(1, count, one, 0)


def span(index, size):
    return pl.ds(pl.multiple_of(index * size, size), size)


def gather_kernel(q, do, k, v, seg, q2, do2, k2, v2, seg2, far_send, far_recv, near_send, near_recv, here):
    me = lax.axis_index("sp")
    core = lax.rem(me, 2)
    row = me // 4
    peer = me + 1 - 2 * core
    greet("sp", me, N_SP)
    mine, theirs = span(core, HALF_Q), span(1 - core, HALF_Q)
    rows = span(me, TOK)
    kv_mine = span(core, HALF_KV)
    local = [
        pltpu.make_async_copy(q.at[:, mine], q2.at[span(core, TOK), :], here.at[0]),
        pltpu.make_async_copy(do.at[:, mine], do2.at[span(core, TOK), :], here.at[1]),
        pltpu.make_async_copy(k.at[:, kv_mine], k2.at[rows, :], here.at[2]),
        pltpu.make_async_copy(v.at[:, kv_mine], v2.at[rows, :], here.at[3]),
        pltpu.make_async_copy(seg, seg2.at[me], here.at[4]),
    ]
    for copy in local:
        copy.start()
    pl.semaphore_wait(pltpu.get_barrier_semaphore(), N_SP - 1)

    def far(src, target):
        lanes = span(lax.rem(target, 2), HALF_KV)
        part = span(src, TOK)
        pairs = (
            (k.at[:, lanes], k2.at[part, :]),
            (v.at[:, lanes], v2.at[part, :]),
            (seg, seg2.at[src]),
        )
        return [
            pltpu.make_async_remote_copy(
                src_ref=a,
                dst_ref=b,
                send_sem=far_send.at[n, target],
                recv_sem=far_recv.at[n, src],
                device_id={"sp": target},
                device_id_type=MESH,
            )
            for n, (a, b) in enumerate(pairs)
        ]

    near = [
        pltpu.make_async_remote_copy(
            src_ref=a.at[:, theirs],
            dst_ref=b.at[span(core, TOK), :],
            send_sem=near_send.at[n],
            recv_sem=near_recv.at[n],
            device_id={"sp": peer},
            device_id_type=MESH,
        )
        for n, (a, b) in enumerate(((q, q2), (do, do2)))
    ]

    def send(d, z):
        target = lax.rem(me + d, N_SP)

        @pl.when(target // 4 >= row)
        def _():
            for copy in far(me, target):
                copy.start()

        return z

    lax.fori_loop(1, N_SP, send, 0)
    for copy in near:
        copy.start()
    for copy in local:
        copy.wait()
    for copy in near:
        copy.wait()

    def finish(d, z):
        other = lax.rem(me + d, N_SP)

        @pl.when(other // 4 >= row)
        def _():
            for copy in far(me, other):
                copy.wait_send()

        @pl.when(other // 4 <= row)
        def _():
            for copy in far(other, me):
                copy.wait_recv()

        return z

    lax.fori_loop(1, N_SP, finish, 0)


def gather(query, grad_out, key, value, seg):
    any_spec = pl.BlockSpec(memory_space=pl.ANY)
    return pl.pallas_call(
        gather_kernel,
        out_shape=(
            jax.ShapeDtypeStruct((ROWS, HALF_Q), bf16),
            jax.ShapeDtypeStruct((ROWS, HALF_Q), bf16),
            jax.ShapeDtypeStruct((SEQ, HALF_KV), bf16),
            jax.ShapeDtypeStruct((SEQ, HALF_KV), bf16),
            jax.ShapeDtypeStruct((N_SP, 1, TOK), jnp.int32),
        ),
        in_specs=[any_spec] * 5,
        out_specs=[any_spec] * 5,
        scratch_shapes=[
            pltpu.SemaphoreType.DMA((3, N_SP)),
            pltpu.SemaphoreType.DMA((3, N_SP)),
            pltpu.SemaphoreType.DMA((2,)),
            pltpu.SemaphoreType.DMA((2,)),
            pltpu.SemaphoreType.DMA((5,)),
        ],
        compiler_params=pltpu.CompilerParams(collective_id=0, has_side_effects=True),
        name="gather_kv_swap_q",
    )(query, grad_out, key, value, seg)


def nt(a, b):
    return lax.dot_general(a, b, (((1,), (1,)), ((), ())), preferred_element_type=f32)


def nn(a, b):
    return lax.dot_general(a, b, (((1,), (0,)), ((), ())), preferred_element_type=f32)


def attend(blocks, chip, q, do, k, v, seg, dq, dk, dv, s_s, e_s, dp_s, dk_s, dv_s, kt, kaug, qoh):
    keys = blocks * KB
    lane = lax.broadcasted_iota(jnp.int32, (TOK, TOK), 1).astype(f32)

    def ids(index):
        line = jnp.broadcast_to(seg[index].astype(f32), (TOK, TOK))
        return line.T

    dk_s[0:keys, :] = jnp.zeros((keys, HALF_KV), f32)
    dv_s[0:keys, :] = jnp.zeros((keys, HALF_KV), f32)
    for h in range(2):
        lanes = slice(h * HEAD_SIZE, (h + 1) * HEAD_SIZE)
        kt[h, :, 0:keys] = k[0:keys, lanes].T
        kaug[h, 0:keys, 0:HEAD_SIZE] = k[0:keys, lanes]
    for n in range(keys // TOK):
        bias = jnp.where(ids(n) == lane, 0.0, NEG).astype(bf16)
        for h in range(2):
            kaug[h, n * TOK : (n + 1) * TOK, HEAD_SIZE:] = bias
    for c in range(2):
        qoh[c * TOK : (c + 1) * TOK, :] = jnp.where(ids(2 * chip + c) == lane, 1.0, 0.0).astype(bf16)
    place = lax.broadcasted_iota(jnp.int32, (KB, WIDE), 0)
    token = lax.broadcasted_iota(jnp.int32, (1, ROWS), 1) + chip * ROWS
    token = jnp.concatenate([token] * HB, axis=1)

    def heads(t, z):
        head = t * HB // GROUP_HEADS
        lanes = span(head, HEAD_SIZE)
        cols = [span(t * HB + j, HEAD_SIZE) for j in range(HB)]
        qt = jnp.concatenate([q[:, c] for c in cols], axis=0)
        dt = jnp.concatenate([do[:, c] for c in cols], axis=0)
        qa = jnp.concatenate([qt, jnp.concatenate([qoh[...]] * HB, axis=0)], axis=1)
        top = None
        for b in range(blocks):
            part = slice(b * KB, (b + 1) * KB)
            s = nt(kaug[head, part, :], qa)
            if b >= blocks - 2:
                s = jnp.where(place + b * KB <= token, s, NEG)
            s_s[part, :] = s
            high = jnp.max(s, axis=0, keepdims=True)
            top = high if top is None else jnp.maximum(top, high)
        total = jnp.zeros((1, WIDE), f32)
        delta = jnp.zeros((1, WIDE), f32)
        for b in range(blocks):
            part = slice(b * KB, (b + 1) * KB)
            dp = nt(v[part, lanes], dt)
            e = jnp.exp2((s_s[part, :] - top) * EXP2_SCALE)
            total = total + jnp.sum(e, axis=0, keepdims=True)
            delta = delta + jnp.sum(e * dp, axis=0, keepdims=True)
            e_s[part, :] = e.astype(bf16)
            dp_s[part, :] = dp.astype(bf16)
        inverse = 1.0 / total
        delta = (delta * inverse).astype(bf16)
        inverse = inverse.astype(bf16)
        acc = None
        for b in range(blocks):
            part = slice(b * KB, (b + 1) * KB)
            p = e_s[part, :] * inverse
            ds = p * (dp_s[part, :] - delta)
            dv_s[part, lanes] += nn(p, dt)
            dk_s[part, lanes] += nn(ds, qt)
            x = nn(kt[head, :, part], ds)
            acc = x if acc is None else acc + x
        out = (acc * SCALE).T.astype(bf16)
        for j in range(HB):
            dq[:, cols[j]] = out[j * ROWS : (j + 1) * ROWS]
        return z

    lax.fori_loop(0, CORE_HEADS // HB, heads, 0)
    dk[0:keys, :] = (dk_s[0:keys, :] * SCALE).astype(bf16)
    dv[0:keys, :] = dv_s[0:keys, :].astype(bf16)


def attention_kernel(*refs):
    me = lax.axis_index("sp")
    chip = me // 2
    for row in range(N_SP // 4):
        pl.when(me // 4 == row)(functools.partial(attend, 2 * (row + 1), chip, *refs))


def attention(q2, do2, k2, v2, seg2):
    vmem = pltpu.VMEM
    spec = pl.BlockSpec(memory_space=vmem)
    return pl.pallas_call(
        attention_kernel,
        out_shape=(
            jax.ShapeDtypeStruct((ROWS, HALF_Q), bf16),
            jax.ShapeDtypeStruct((SEQ, HALF_KV), bf16),
            jax.ShapeDtypeStruct((SEQ, HALF_KV), bf16),
        ),
        in_specs=[spec] * 5,
        out_specs=[spec] * 3,
        scratch_shapes=[
            vmem((SEQ, WIDE), f32),
            vmem((SEQ, WIDE), bf16),
            vmem((SEQ, WIDE), bf16),
            vmem((SEQ, HALF_KV), f32),
            vmem((SEQ, HALF_KV), f32),
            vmem((2, HEAD_SIZE, SEQ), bf16),
            vmem((2, SEQ, 2 * HEAD_SIZE), bf16),
            vmem((ROWS, HEAD_SIZE), bf16),
        ],
        compiler_params=pltpu.CompilerParams(vmem_limit_bytes=58 << 20),
        name="attention_grads",
    )(q2, do2, k2, v2, seg2)


def finish_kernel(
    dq, dk, dv, gq, gk, gv, dq_in, dk_in, dv_in, k_sum, v_sum, sq_mine, sq_sp, sq_grp,
    near_send, near_recv, far_send, far_recv, here, sp_send, sp_recv, grp_send, grp_recv,
):
    me = lax.axis_index("sp")
    group = lax.axis_index("grp")
    core = lax.rem(me, 2)
    chip = me // 2
    peer = me + 1 - 2 * core
    greet("sp", me, N_SP)
    greet("grp", group, N_GRP)
    pl.semaphore_wait(pltpu.get_barrier_semaphore(), N_SP + N_GRP - 2)

    def far(src, target):
        part = span(target, TOK)
        return [
            pltpu.make_async_remote_copy(
                src_ref=a.at[part, :],
                dst_ref=b.at[src],
                send_sem=far_send.at[n, target],
                recv_sem=far_recv.at[n, src],
                device_id={"sp": target},
                device_id_type=MESH,
            )
            for n, (a, b) in enumerate(((dk, dk_in), (dv, dv_in)))
        ]

    near = pltpu.make_async_remote_copy(
        src_ref=dq.at[span(1 - core, TOK), :],
        dst_ref=dq_in,
        send_sem=near_send,
        recv_sem=near_recv,
        device_id={"sp": peer},
        device_id_type=MESH,
    )
    local = [
        pltpu.make_async_copy(dk.at[span(me, TOK), :], dk_in.at[me], here.at[0]),
        pltpu.make_async_copy(dv.at[span(me, TOK), :], dv_in.at[me], here.at[1]),
    ]

    def send(d, z):
        target = lax.rem(me + d, N_SP)

        @pl.when(target // 2 <= chip)
        def _():
            for copy in far(me, target):
                copy.start()

        return z

    lax.fori_loop(1, N_SP, send, 0)
    near.start()
    for copy in local:
        copy.start()
    for copy in local:
        copy.wait()

    def square(x):
        x = x.astype(f32)
        return jnp.sum(x * x)

    own = dq.at[span(core, TOK), :]
    squares = square(own[...])
    near.wait()
    squares += square(dq_in[...])

    def arrive(d, z):
        other = lax.rem(me + d, N_SP)

        @pl.when(other // 2 >= chip)
        def _():
            for copy in far(other, me):
                copy.wait_recv()

        @pl.when(other // 2 <= chip)
        def _():
            for copy in far(me, other):
                copy.wait_send()

        return z

    lax.fori_loop(1, N_SP, arrive, 0)
    k_sum[...] = jnp.zeros_like(k_sum)
    v_sum[...] = jnp.zeros_like(v_sum)

    def add(j, z):
        for c in range(2):
            lanes = slice(c * HALF_KV, (c + 1) * HALF_KV)
            k_sum[:, lanes] += dk_in[2 * j + c].astype(f32)
            v_sum[:, lanes] += dv_in[2 * j + c].astype(f32)
        return z

    lax.fori_loop(chip, N_SP // 2, add, 0)
    squares += square(k_sum[...]) + square(v_sum[...])
    for axis, index, count, slots, sends, recvs in (
        ("sp", me, N_SP, sq_sp, sp_send, sp_recv),
        ("grp", group, N_GRP, sq_grp, grp_send, grp_recv),
    ):
        stage = 0 if axis == "sp" else 1
        sq_mine[stage] = jnp.full((8, 128), squares, f32)

        def message(src, target):
            return pltpu.make_async_remote_copy(
                src_ref=sq_mine.at[stage],
                dst_ref=slots.at[src],
                send_sem=sends.at[target],
                recv_sem=recvs.at[src],
                device_id={axis: target},
                device_id_type=MESH,
            )

        def start(d, z):
            message(index, lax.rem(index + d, count)).start()
            return z

        def wait(d, z):
            other = lax.rem(index + d, count)
            message(index, other).wait_send()
            message(other, index).wait_recv()
            return z

        lax.fori_loop(1, count, start, 0)
        slots[index] = sq_mine[stage]
        lax.fori_loop(1, count, wait, 0)
        tile = jnp.sum(slots[...], axis=0)
        squares = jnp.max(tile)
    factor = 1.0 / jnp.sqrt(jnp.full((8, 128), squares, f32) / ITEMS + 1e-6)
    factor = factor[0:1, 0:1]
    gq[:, span(core, HALF_Q)] = (own[...].astype(f32) * factor).astype(bf16)
    gq[:, span(1 - core, HALF_Q)] = (dq_in[...].astype(f32) * factor).astype(bf16)
    gk[...] = (k_sum[...] * factor).astype(bf16)
    gv[...] = (v_sum[...] * factor).astype(bf16)


def finish(dq, dk, dv):
    vmem = pltpu.VMEM
    spec = pl.BlockSpec(memory_space=vmem)
    sems = pltpu.SemaphoreType.DMA
    width = KEY_VALUE_HEADS * HEAD_SIZE
    return pl.pallas_call(
        finish_kernel,
        out_shape=(
            jax.ShapeDtypeStruct((TOK, QUERY_HEADS * HEAD_SIZE), bf16),
            jax.ShapeDtypeStruct((TOK, width), bf16),
            jax.ShapeDtypeStruct((TOK, width), bf16),
        ),
        in_specs=[spec] * 3,
        out_specs=[spec] * 3,
        scratch_shapes=[
            vmem((TOK, HALF_Q), bf16),
            vmem((N_SP, TOK, HALF_KV), bf16),
            vmem((N_SP, TOK, HALF_KV), bf16),
            vmem((TOK, width), f32),
            vmem((TOK, width), f32),
            vmem((2, 8, 128), f32),
            vmem((N_SP, 8, 128), f32),
            vmem((N_GRP, 8, 128), f32),
            sems(()),
            sems(()),
            sems((2, N_SP)),
            sems((2, N_SP)),
            sems((2,)),
            sems((N_SP,)),
            sems((N_SP,)),
            sems((N_GRP,)),
            sems((N_GRP,)),
        ],
        compiler_params=pltpu.CompilerParams(
            collective_id=1, has_side_effects=True, vmem_limit_bytes=40 << 20
        ),
        name="reduce_and_scale",
    )(dq, dk, dv)


def on_device(query, key, value, grad_out, segment_ids):
    moved = gather(query, grad_out, key, value, segment_ids.reshape(1, TOK))
    return finish(*attention(*moved))


def solution(mesh):
    whole = P(("grp", "sp"), None)
    return jax.shard_map(
        on_device,
        mesh=mesh,
        in_specs=(whole, whole, whole, whole, P(("grp", "sp"))),
        out_specs=(whole, whole, whole),
        check_vma=False,
    )
```

time: 393 us -> 157 us (0.40); the launches traced: 388 us -> 157 us
  Pallas kernels: 0 us -> 150 us
  blocking collectives: 111 us -> 0 us
  waiting for transfers between devices: 77.2 us -> 0 us
  matrix products: 74.8 us -> 0 us
  other arithmetic: 46.3 us -> 0 us
  local copies, waits for them, and re-layouts: 34.3 us -> 6.31 us
  starting transfers between devices: 27.2 us -> 0 us
  between operations: 17.5 us -> 0.65 us
    pallas_call x0 -> x3, Pallas kernels: none -> 150 us  [the longest x1 78.2 us: finish(): pl.pallas_call(finish_kernel, out_shape=(jax.ShapeDtypeStruct((TOK, QUERY...]
    psum x1 -> x0, blocking collectives: 75.6 us -> none  [on_device(): total = lax.psum(local, ('grp', 'sp'))]
    dot_general x21 -> x0, matrix products: 54.5 us -> none  [the longest x4 13.4 us: block_grads(): dprob = jnp.einsum('qhd,kd->hqk', dob, vw, preferred_element_type=f32)]
    all_gather x2 -> x0, waiting for transfers between devices: 43.6 us -> none  [the longest x1 43.6 us: on_device(): lax.all_gather(value, 'sp', axis=0, tiled=True)]
    all_gather x1 -> x0, blocking collectives: 35.2 us -> none  [on_device(): seg_seq = lax.all_gather(segment_ids, 'sp', axis=0, tiled=True)]
    all_to_all x5 -> x0, waiting for transfers between devices: 32.2 us -> none  [the longest x1 14.4 us: on_device(): lax.all_to_all(q_low, 'sp', split_axis=0, concat_axis=1, tiled=True)]
    all_to_all x5 -> x0, starting transfers between devices: 27.2 us -> none  [the longest x1 8.58 us: on_device(): lax.all_to_all(q_split, 'sp', split_axis=1, concat_axis=0, tiled=True)]
    convert_element_type x7 -> x0, other arithmetic: 22.9 us -> none  [the longest x4 17.8 us: block_grads(): prob_low = prob.astype(jnp.bfloat16)]
  transfers between devices with their start and end apart: 7 -> 0, of which waited for: 5 -> 0; matrix products, arithmetic and copies ran while one was open for 15% -> 0% of each run, Pallas kernels for 0% -> 0%
where the time goes in v1:
time: 157 us
  Pallas kernels  150 us (96%)
  local copies, waits for them, and re-layouts  6.31 us (4%)
    pallas_call x1, Pallas kernels, finish(): pl.pallas_call(finish_kernel, out_shape=(jax.ShapeDtypeStruct((TOK, QUERY...  78.2 us
    pallas_call x1, Pallas kernels, gather(): pl.pallas_call(gather_kernel, out_shape=(jax.ShapeDtypeStruct((ROWS, HALF...  54.5 us
    pallas_call x1, Pallas kernels, attention(): pl.pallas_call(attention_kernel, out_shape=(jax.ShapeDtypeStruct((ROWS, H...  17.1 us
    unnamed x9, local copies, waits for them, and re-layouts  6.31 us

profile of v1, /device:TPU:1, one launch (start us, length us, event | category | flops | bytes accessed | tf_op | source)
XLA Modules:
  0.0 156.7 jit_solution(925778437344543151)
XLA Ops:
  0.6 54.5 %gather_kv_swap_q.1 = (bf16[256,3072]{1,0:T(8,128)(2,1)}, bf16[256,3072]{1,0:T(8,128)(2,1)}, bf16[2048,256]{1,0:T(8,128)(2,1)}, bf16[2048,256]{1,0:T(8,128)(2,1)}, s32[16,1,128]{2,1,0:T(1,128)}) custom-call(bf16[128,6144]{1,0:T(8,128)(2,1)} %q.1, bf16[128,6144]{1,0:T(8,128)(2,1)} %do.1, bf16[128,512]{1,0:T(8,128)(2,1)} %k.1, bf16[128,512]{1,0:T(8,128)(2,1)} %v.1, ...), custom_call_target="tpu_custom_call" | custom-call | tf_op jit(solution)/shard_map/gather_kv_swap_q/pallas_call | solution.py:140
  55.1 17.1 %attention_grads.1 = (bf16[256,3072]{1,0:T(8,128)(2,1)}, bf16[2048,256]{1,0:T(8,128)(2,1)}, bf16[2048,256]{1,0:T(8,128)(2,1)}) custom-call(bf16[256,3072]{1,0:T(8,128)(2,1)} %get-tuple-element.11.refs_0_, bf16[256,3072]{1,0:T(8,128)(2,1)} %get-tuple-element.12.refs_1_, bf16[2048,256]{1,0:T(8,128)(2,1)} %get-tuple-element.13.refs_2_, ...), custom_call_target="tpu_custom_call" | custom-call | tf_op jit(solution)/shard_map/attention_grads/pallas_call | solution.py:253
  72.2 0.0 copy-start
  72.2 1.4 copy-done
  73.6 0.0 copy-start.1
  73.6 1.2 copy-done.1
  74.8 0.0 copy-start.2
  74.8 1.2 copy-done.2
  76.1 78.2 %reduce_and_scale.1 = (bf16[128,6144]{1,0:T(8,128)(2,1)S(1)}, bf16[128,512]{1,0:T(8,128)(2,1)S(1)}, bf16[128,512]{1,0:T(8,128)(2,1)S(1)}) custom-call(bf16[256,3072]{1,0:T(8,128)(2,1)S(1)} %copy-done, bf16[2048,256]{1,0:T(8,128)(2,1)S(1)} %copy-done.1, bf16[2048,256]{1,0:T(8,128)(2,1)S(1)} %copy-done.2), custom_call_target="tpu_custom_call" | custom-call | tf_op jit(solution)/shard_map/reduce_and_scale/pallas_call | solution.py:416
  154.2 1.1 copy.11
  155.4 0.7 copy.12
  156.1 0.7 copy.13
Async XLA Ops:
  72.2 1.4 copy-start
  73.6 1.2 copy-start.1
  74.8 1.2 copy-start.2
